TPU v7x, 128 devices: a whole 4x4x4 slice. The times are simulated.
128 devices in a mesh: ctx: 16 (over x, y_hi, core), head: 8 (over y_lo, z).
Axes of the slice: x: 4, y: 4 (y_hi: 2, y_lo: 2; y = y_hi * 2 + y_lo), z: 4, core: 2. Of those that a mesh axis runs over, the one named last changes fastest.
Arguments:
- queries: bfloat16 [4096, 8192], P('ctx', 'head'), may hold values from -64 to 64
- upstream: bfloat16 [4096, 8192], P('ctx', 'head'), may hold values from -12 to 12
- key_value: bfloat16 [4096, 1024], P('ctx', 'head'), may hold values from -6 to 6
- doc_ids: int32 [4096], replicated, may hold values from 0 to 3, never falling along the last dimension, each value on 1 to 2048 neighbouring positions
- seq_weight: float32 [4], replicated, may hold values from -2 to 2
Outputs:
- query_grad: bfloat16 [4096, 8192], P('ctx', 'head')
- kv_grad: bfloat16 [4096, 1024], P('ctx', 'head')
Inputs may be any that keep to these rules, and one draw needn't show every extreme that they name: `doc_ids`: document numbers never fall along the slab; each of the 4 documents holds 1 to 2048 positions, and one holds exactly 2048.
All inputs are finite; a program needn't handle non-finite values.
Results may differ from a plain program's by a relative error of at most 0.0058.
Values may be sent and summed in bfloat16 or wider, within the bound.
A program may use at most 64 MiB of HBM per device.

v0:
```python
import math

import jax
import jax.numpy as jnp
from jax import lax
from jax.sharding import PartitionSpec as P

KV_HEADS = 4
HEAD = 128


NEG_FILL = -1e30


def partner_2(value, axis, stride):
    mask = 2**stride
    pairs = [(source, source ^ mask) for source in range(lax.axis_size(axis))]
    return lax.ppermute(value, axis, pairs)


def row_weights(row_docs, seq_weight):
    labels = jnp.arange(seq_weight.shape[0], dtype=jnp.int32)
    return jnp.sum(
        jnp.where(row_docs[:, None] == labels[None, :], seq_weight[None, :], 0.0), axis=1
    )


def visibility(row_start, row_count, key_start, key_width, doc_ids):
    row_pos = row_start + jnp.arange(row_count, dtype=jnp.int32)
    key_pos = key_start + jnp.arange(key_width, dtype=jnp.int32)
    row_docs = lax.dynamic_slice_in_dim(doc_ids, row_start, row_count, 0)
    key_docs = lax.dynamic_slice_in_dim(doc_ids, key_start, key_width, 0)
    return (row_docs[:, None] == key_docs[None, :]) & (key_pos[None, :] <= row_pos[:, None])


def spread_heads(block_cols, head_index, mover):
    partner = mover(block_cols, 0)
    upper_bit = head_index >> 0 & 1 == 1
    block_cols = jnp.where(
        upper_bit,
        jnp.concatenate([partner, block_cols], 1),
        jnp.concatenate([block_cols, partner], 1),
    )
    return block_cols


def halve_heads(kv_term, head_index, group_steps, mover):
    for bit_number in reversed(range(group_steps)):
        half_cols = kv_term.shape[1] // 2
        lower_half = kv_term[:, :half_cols]
        upper_half = kv_term[:, half_cols:]
        high_bit = head_index >> bit_number & 1 == 1
        kept_half = jnp.where(high_bit, upper_half, lower_half)
        sent_half = jnp.where(high_bit, lower_half, upper_half)
        kv_term = kept_half + mover(sent_half, bit_number)
    return kv_term


def segment_grads(query_rows, upstream_rows, row_start, keys, values, doc_ids, kv_term, key_block):
    row_count = query_rows.shape[0]
    head_count = query_rows.shape[1] // HEAD
    query_heads = query_rows.reshape(row_count, head_count, HEAD)
    upstream_heads = upstream_rows.reshape(row_count, head_count, HEAD)
    score_scale = 1.0 / math.sqrt(HEAD)
    needed_blocks = (row_start + row_count - 1) // key_block + 1

    def scores_at(block_index):
        key_start = block_index * key_block
        key_tile = lax.dynamic_slice_in_dim(keys, key_start, key_block, 0)
        value_tile = lax.dynamic_slice_in_dim(values, key_start, key_block, 0)
        visible = visibility(row_start, row_count, key_start, key_block, doc_ids)[None, :, :]
        scores = (
            jnp.einsum("nhd,kd->hnk", query_heads, key_tile, preferred_element_type=jnp.float32)
            * score_scale
        )
        return (key_start, key_tile, value_tile, visible, jnp.where(visible, scores, NEG_FILL))

    def stats_step(block_index, state_pair):
        run_top, run_total = state_pair
        key_start, key_tile, value_tile, visible, scores = scores_at(block_index)
        new_top = jnp.maximum(run_top, jnp.max(scores, axis=2))
        shifted = jnp.where(visible, jnp.exp(scores - new_top[:, :, None]), 0.0)
        run_total = run_total * jnp.exp(run_top - new_top) + jnp.sum(shifted, axis=2)
        return (new_top, run_total)

    start_pair = (
        jnp.full((head_count, row_count), NEG_FILL, jnp.float32),
        jnp.zeros((head_count, row_count), jnp.float32),
    )
    run_top, run_total = lax.fori_loop(0, needed_blocks, stats_step, start_pair)
    log_total = run_top + jnp.log(run_total)

    def probs_at(block_index):
        key_start, key_tile, value_tile, visible, scores = scores_at(block_index)
        probs = jnp.where(visible, jnp.exp(scores - log_total[:, :, None]), 0.0)
        grad_probs = jnp.einsum(
            "nhd,kd->hnk", upstream_heads, value_tile, preferred_element_type=jnp.float32
        )
        return (key_start, key_tile, probs, grad_probs)

    def delta_step(block_index, row_delta):
        key_start, key_tile, probs, grad_probs = probs_at(block_index)
        return row_delta + jnp.sum(probs * grad_probs, axis=2)

    row_delta = lax.fori_loop(
        0, needed_blocks, delta_step, jnp.zeros((head_count, row_count), jnp.float32)
    )

    def grad_step(block_index, state_pair):
        grad_query, term_now = state_pair
        key_start, key_tile, probs, grad_probs = probs_at(block_index)
        grad_scores = (probs * (grad_probs - row_delta[:, :, None])).astype(jnp.bfloat16)
        probs_bf16 = probs.astype(jnp.bfloat16)
        grad_query = (
            grad_query
            + jnp.einsum("hnk,kd->nhd", grad_scores, key_tile, preferred_element_type=jnp.float32)
            * score_scale
        )
        grad_key = (
            jnp.einsum("hnk,nhd->kd", grad_scores, query_heads, preferred_element_type=jnp.float32)
            * score_scale
        )
        grad_value = jnp.einsum(
            "hnk,nhd->kd", probs_bf16, upstream_heads, preferred_element_type=jnp.float32
        )
        current = lax.dynamic_slice_in_dim(term_now, key_start, key_block, 0)
        term_now = lax.dynamic_update_slice_in_dim(
            term_now, current + jnp.concatenate([grad_key, grad_value], 1), key_start, 0
        )
        return (grad_query, term_now)

    start_grad = jnp.zeros((row_count, head_count, HEAD), jnp.float32)
    grad_query, kv_term = lax.fori_loop(0, needed_blocks, grad_step, (start_grad, kv_term))
    return (grad_query.reshape(row_count, head_count * HEAD), kv_term)


def per_device(queries, upstream, key_value, doc_ids, seq_weight):
    row_total = queries.shape[0]
    ctx_count = lax.axis_size("ctx")
    slab_rows = row_total * ctx_count
    group_size = lax.axis_size("head") // KV_HEADS
    group_steps = group_size.bit_length() - 1
    ctx_index = lax.axis_index("ctx")
    head_index = lax.axis_index("head")
    key_block = min(512, slab_rows)
    own_start = ctx_index * row_total
    weights_rows = row_weights(
        lax.dynamic_slice_in_dim(doc_ids, own_start, row_total, 0), seq_weight
    )
    weighted = (upstream.astype(jnp.float32) * weights_rows[:, None]).astype(jnp.bfloat16)
    whole_head = spread_heads(
        key_value, head_index, lambda piece, bit_number: partner_2(piece, "head", bit_number)
    )
    key_values = lax.all_gather(whole_head, "ctx", axis=0, tiled=True)
    keys = key_values[:, :HEAD]
    values = key_values[:, HEAD:]
    kv_term = jnp.zeros((slab_rows, 2 * HEAD), jnp.float32)
    own_grad, kv_term = segment_grads(
        queries, weighted, own_start, keys, values, doc_ids, kv_term, key_block
    )
    query_grad = own_grad.astype(jnp.bfloat16)
    summed = lax.psum_scatter(kv_term, "ctx", scatter_dimension=0, tiled=True)
    kv_grad = halve_heads(
        summed,
        head_index,
        group_steps,
        lambda piece, bit_number: partner_2(piece, "head", bit_number),
    )
    return (query_grad, kv_grad.astype(jnp.bfloat16))


def solution(mesh):
    return jax.shard_map(
        per_device,
        mesh=mesh,
        in_specs=(P("ctx", "head"), P("ctx", "head"), P("ctx", "head"), P(), P()),
        out_specs=(P("ctx", "head"), P("ctx", "head")),
        check_vma=False,
    )
```

profile of v0, /device:TPU:2, one launch (start us, length us, event | category | flops | bytes accessed | tf_op | source)
XLA Modules:
  0.0 385.0 jit_solution(13803664419639619137)
XLA Ops:
  7.2 2.0 collective-permute-start
  9.2 2.6 collective-permute-done
  11.8 1.6 maximum_select_fusion
  13.4 1.2 copy.26
  15.0 0.8 dynamic_slice.57
  16.5 1.2 multiply_convert_fusion
  18.2 45.8 %all-gather.2.cloned.1.call-done = bf16[4096,256]{1,0:T(8,128)(2,1)} async-done(((bf16[256,256]{1,0:T(8,128)(2,1)}), bf16[4096,256]{1,0:T(8,128)(2,1)}) %all-gather.2.cloned.1.call-update) | async-done | bytes 2097168 | tf_op jit(solution)/shard_map/all_gather | solution.py:154
  64.0 3.0 fusion.44
  67.0 11.2 %while.40 = (s32[]{:T(128)}, f32[8,256]{1,0:T(8,128)S(1)}, f32[8,256]{1,0:T(8,128)S(1)}, s32[]{:T(128)}, s32[256]{0:T(256)S(1)}, /*index=5*/s32[4096]{0:T(1024)}...) while((s32[]{:T(128)}, f32[8,256]{1,0:T(8,128)S(1)}, ...), condition=%wide.region_3.4_spmd, body=%wide.region_0.3_spmd.sunk | while | flops 277222144 | bytes 9557179 | solution.py:90
  68.0 1.7 fusion.78
  69.7 1.0 select_reduce_fusion.3
  70.8 0.8 dynamic_slice.96
  71.7 1.7 fusion.78
  73.4 1.0 select_reduce_fusion.3
  74.5 0.8 dynamic_slice.96
  75.5 1.7 fusion.78
  77.2 1.0 select_reduce_fusion.3
  78.3 15.1 %while.41 = (s32[]{:T(128)}, f32[8,256]{1,0:T(8,128)S(1)}, s32[]{:T(128)}, s32[256]{0:T(256)S(1)}, s32[4096]{0:T(1024)}, /*index=5*/s32[]{:T(128)}, bf16[4096,12...) while((s32[]{:T(128)}, f32[8,256]{1,0:T(8,128)S(1)}, ...), condition=%wide.region_7.8_spmd, body=%wide.region_5.7_spmd.sunk | while | flops 543556352 | bytes 10015951 | solution.py:105
  78.3 0.8 dynamic_slice.99
  79.3 1.6 fusion.83
  80.9 2.4 fusion.84
  84.3 1.6 fusion.83
  85.9 2.4 fusion.84
  89.3 1.6 fusion.83
  91.0 2.4 fusion.84
  93.4 2.2 broadcast_in_dim.112.clone
  95.6 1.1 broadcast_in_dim.111
  96.7 56.4 %while.42 = (s32[]{:T(128)}, f32[256,8,128]{0,2,1:T(8,128)}, f32[4096,256]{1,0:T(8,128)}, s32[]{:T(128)}, bf16[4096,128]{1,0:T(8,128)(2,1)}, /*index=5*/s32[256]...) while((s32[]{:T(128)}, f32[256,8,128]{0,2,1:T(8,128)}, ...), condition=%wide.region_9.10_spmd, body=%wide.region_8.9_spmd.sunk | while | flops 1356006144 | bytes 34379040 | solution.py:133
  97.6 1.6 fusion.95
  99.3 2.4 fusion.96
  101.7 0.8 fusion.99
  102.5 3.2 fusion.98
  105.7 1.9 constant_dynamic-slice_fusion.2
  107.5 1.2 copy.47
  108.8 1.8 maximum_add_fusion.2
  110.6 1.2 copy.48
  111.8 0.8 constant_dynamic-update-slice_fusion.2
  112.7 2.8 fusion.97
  116.5 1.6 fusion.95
  118.1 2.4 fusion.96
  120.5 0.8 fusion.99
  121.3 3.2 fusion.98
  124.5 1.9 constant_dynamic-slice_fusion.2
  126.3 1.2 copy.47
  127.6 1.8 maximum_add_fusion.2
  129.4 1.2 copy.48
  130.6 0.8 constant_dynamic-update-slice_fusion.2
  131.5 2.8 fusion.97
  135.3 1.6 fusion.95
  136.9 2.4 fusion.96
  139.3 0.8 fusion.99
  140.1 3.2 fusion.98
  143.3 1.9 constant_dynamic-slice_fusion.2
  145.1 1.2 copy.47
  146.4 1.8 maximum_add_fusion.2
  148.2 1.2 copy.48
  149.4 0.8 constant_dynamic-update-slice_fusion.2
  150.3 2.8 fusion.97
  153.1 217.4 %reduce-scatter.2.cloned.1.call-done = f32[256,256]{1,0:T(8,128)} async-done(((f32[4096,256]{1,0:T(8,128)}), f32[256,256]{1,0:T(8,128)}) %reduce-scatter.2.cloned.1.call-update) | async-done | bytes 262160 | tf_op jit(solution)/shard_map/reduce_scatter | solution.py:162
  370.5 1.0 slice_select_fusion
  371.5 1.7 collective-permute-start.1
  373.2 1.0 copy.40
  374.2 2.3 collective-permute-done.1
  376.6 1.6 add_convert_fusion
  (72 shorter events, 8.2 us)
Async XLA Ops:
  7.2 56.8 %all-gather.2.cloned.1.call-start = ((), (), s32[]{:S(2)}) async-start(), calls=%async_computation.1 | async-start | bytes 2228224 | tf_op jit(solution)/shard_map/all_gather | solution.py:154
  7.2 4.6 %collective-permute-start = (bf16[256,128]{1,0:T(8,128)(2,1)}, bf16[256,128]{1,0:T(8,128)(2,1)S(1)}, u32[]{:S(2)}, u32[]{:S(2)}) collective-permute-start(bf16[256,128]{1,0:T(8,128)(2,1)} %param.13), channel_id=1, source_target_pairs={{0,1},{1,0},{2,3},{3,2},{4,5},{5,4},{6,7},{7,6},{8,9},{9,8},{10,11... | collective-permute-start | bytes 196616 | tf_op jit(solution)/shard_map/ppermute | solution.py:18
  13.4 357.1 %reduce-scatter.2.cloned.1.call-start = ((), (), s32[]{:S(2)}) async-start(), calls=%async_computation.2 | async-start | bytes 4456448 | tf_op jit(solution)/shard_map/reduce_scatter | solution.py:162
  96.7 2.6 copy-start.1
  112.7 2.8 copy-start.2
  115.5 2.6 copy-start.1
  131.5 2.8 copy-start.2
  134.3 2.6 copy-start.1
  150.3 2.8 copy-start.2
  153.1 220.1 %copy-start = (f32[256,8,128]{0,2,1:T(8,128)S(1)}, f32[256,8,128]{0,2,1:T(8,128)}, u32[]{:S(2)}) copy-start(f32[256,8,128]{0,2,1:T(8,128)} %get-tuple-element.388) | copy-start | bytes 3145732
  371.5 5.0 %collective-permute-start.1 = (f32[256,128]{1,0:T(8,128)S(1)}, f32[256,128]{1,0:T(8,128)S(1)}, u32[]{:S(2)}, u32[]{:S(2)}) collective-permute-start(f32[256,128]{1,0:T(8,128)S(1)} %slice_select_fusion), channel_id=1, source_target_pairs={{0,1},{1,0},{2,3},{3,2},{4,5},{5,4},{6,7},{7,6},{8,9},{9,8},{10,11... | collective-permute-start | bytes 393224 | tf_op jit(solution)/shard_map/ppermute | solution.py:18
Sparse Core Ops, SparseCore 0:
  13.5 50.4 all-gather.1
  153.3 217.2 reduce-scatter.1
where the time goes:
time: 389 us; the launch traced here: 385 us
  waiting for transfers between devices  268 us (69%)
  matrix products  49.4 us (13%)
  local copies, waits for them, and re-layouts  32.5 us (8%)
  other arithmetic  16.6 us (4%)
  between operations  14.1 us (4%)
    reduce_scatter x1, waiting for transfers between devices, per_device(): summed = lax.psum_scatter(kv_term, 'ctx', scatter_dimension=0, tiled=True)  217 us
    all_gather x1, waiting for transfers between devices, per_device(): key_values = lax.all_gather(whole_head, 'ctx', axis=0, tiled=True)  45.8 us
    dot_general x9, matrix products, scores_at(): jnp.einsum('nhd,kd->hnk', query_heads, key_tile, preferred_element_type=j...  14.7 us
    dot_general x6, matrix products, probs_at(): jnp.einsum('nhd,kd->hnk', upstream_heads, value_tile, preferred_element_t...  14.3 us
    dot_general x3, matrix products, grad_step(): jnp.einsum('hnk,nhd->kd', probs_bf16, upstream_heads, preferred_element_t...  9.52 us
    dynamic_slice x6, local copies, waits for them, and re-layouts, grad_step(): current = lax.dynamic_slice_in_dim(term_now, key_start, key_block, 0)  9.31 us
    dot_general x3, matrix products, grad_step(): jnp.einsum('hnk,kd->nhd', grad_scores, key_tile, preferred_element_type=j...  8.45 us
  transfers between devices with their start and end apart: 4, of which 4 were waited for; matrix products, arithmetic and copies ran while one was open for 1% of the time, Pallas kernels for 0%

commit v1 on v0

v1 whole, which is shorter than its diff:
```python
import functools
import math

import jax
import jax.numpy as jnp
from jax import lax
from jax.experimental import pallas as pl
from jax.experimental.pallas import tpu as pltpu
from jax.sharding import PartitionSpec as P

HEAD = 128
PAIRS = 4
LOG2_SCALE = math.log2(math.e) / math.sqrt(HEAD)
SCALE = 1.0 / math.sqrt(HEAD)
BIG = 1e30
MESH = pl.DeviceIdType.MESH
F32 = jnp.float32
BF16 = jnp.bfloat16


def kernel(rows, heads, chips, docs_n, *refs):
    (
        q_ref, up_ref, kv_ref, docs_ref, weight_ref, dq_ref, dkv_ref,
        q_t, up_t, q_n, up_n, window, keys_x, keys_t, p_a, p_b, dp_a, dp_b, p16, grad_s,
        top_ref, snap_ref, total_ref, delta_ref,
        part, sib_out, sib_in, kept, z_out, z_in, far_out, far_in,
        gd_send, gd_recv, gz_send, gz_recv, gs_send, gs_recv,
        rs_send, rs_recv, rz_send, rz_recv, rd_send, rd_recv,
    ) = refs
    ctx = lax.axis_index("ctx")
    head = lax.axis_index("head")
    chip = ctx // 2
    core = ctx % 2
    half = head % 2
    sibling = (ctx + 1 - 2 * core, head)
    z_mate = (ctx, head + 1 - 2 * half)
    lines = rows // 128
    all_rows = heads * rows

    def later(e):
        return (ctx + 2 * e, head)

    def earlier(e):
        return (ctx - 2 * e, head)

    def copy(src, dst, send, recv, to):
        return pltpu.make_async_remote_copy(
            src_ref=src, dst_ref=dst, send_sem=send, recv_sem=recv, device_id=to, device_id_type=MESH
        )

    def give_far(e):
        return copy(kv_ref, window.at[2 * e, half], gd_send.at[e - 1], gd_recv.at[e - 1], later(e))

    def give_z(e):
        src = kv_ref if e == 0 else window.at[2 * e, half]
        return copy(src, window.at[2 * e, half], gz_send.at[e], gz_recv.at[e], z_mate)

    def give_sibling(e, which, own):
        src = kv_ref if own and e == 0 else window.at[2 * e, which]
        slot = 0 if own else 1
        return copy(
            src, window.at[2 * e + 1 - 2 * core, which],
            gs_send.at[e, slot], gs_recv.at[e - core, slot], sibling,
        )

    def sibling_wants(e):
        first = chip >= e
        if e == 0:
            return core == 0
        if e == PAIRS:
            return jnp.logical_and(first, core == 1)
        return first

    def send_sibling(t):
        return copy(sib_out.at[t - 1], sib_in.at[t - core], rs_send.at[t - 1], rs_recv.at[t - core], sibling)

    def send_z(e):
        return copy(z_out.at[e], z_in.at[e], rz_send.at[e], rz_recv.at[e], z_mate)

    def send_far(e):
        return copy(far_out.at[e - 1], far_in.at[e - 1], rd_send.at[e - 1], rd_recv.at[e - 1], earlier(e))

    def has_sibling_term(e):
        if e == 0:
            return core == 0
        if e == PAIRS:
            return core == 1
        return None

    barrier = pltpu.get_barrier_semaphore()
    pl.semaphore_signal(barrier, inc=1, device_id=sibling, device_id_type=MESH)
    pl.semaphore_signal(barrier, inc=1, device_id=z_mate, device_id_type=MESH)
    for e in range(1, PAIRS + 1):
        @pl.when(chip + e < chips)
        def _():
            pl.semaphore_signal(barrier, inc=1, device_id=later(e), device_id_type=MESH)

        @pl.when(chip >= e)
        def _():
            pl.semaphore_signal(barrier, inc=1, device_id=earlier(e), device_id_type=MESH)

    pl.semaphore_wait(barrier, 2 + jnp.minimum(PAIRS, chips - 1 - chip) + jnp.minimum(PAIRS, chip))

    give_z(0).start()

    @pl.when(core == 0)
    def _():
        give_sibling(0, half, True).start()

    for e in range(1, PAIRS + 1):
        @pl.when(chip + e < chips)
        def _():
            give_far(e).start()

    window[0, half] = kv_ref[...]

    def doc_line(block):
        at = jnp.maximum(block, 0) * lines
        return jnp.concatenate([docs_ref[pl.ds(at + i, 1), :] for i in range(lines)], axis=1)

    sub = lax.broadcasted_iota(jnp.int32, (HEAD, rows), 0)
    row_docs = doc_line(ctx)
    row_weight = jnp.zeros((1, rows), F32)
    for d in range(docs_n):
        row_weight = row_weight + jnp.where(row_docs == d, weight_ref[d], 0.0)
    column_weight = jnp.broadcast_to(row_weight, (HEAD, rows)).T
    ban = jnp.where((sub < docs_n + 1) & (sub != row_docs), -BIG, 0.0).astype(BF16)
    for h in range(heads):
        cols = slice(h * HEAD, (h + 1) * HEAD)
        span = slice(h * rows, (h + 1) * rows)
        q_here = q_ref[:, cols]
        q_n[span, :] = q_here
        q_t[:HEAD, span] = q_here.T
        q_t[HEAD:, span] = ban
        weighted = (up_ref[:, cols].astype(F32) * column_weight).astype(BF16)
        up_n[span, :] = weighted
        up_t[:, span] = weighted.T
    for d in range(2 * PAIRS + 1):
        key_docs = jnp.where(ctx >= d, doc_line(ctx - d), docs_n)
        keys_x[d * rows:(d + 1) * rows, HEAD:] = jnp.where(sub == key_docs, 1.0, 0.0).astype(BF16).T

    def relay_far(e):
        @pl.when(chip >= e)
        def _():
            give_far(e).wait_recv()
            give_z(e).start()

        @pl.when(sibling_wants(e))
        def _():
            give_sibling(e, half, True).start()

    def relay_z(e):
        @pl.when(chip >= e)
        def _():
            give_z(e).wait_recv()

        @pl.when(sibling_wants(e))
        def _():
            give_sibling(e, 1 - half, False).start()

    def await_sibling(t):
        for slot in range(2):
            copy(
                kv_ref, window.at[2 * t - 1, 0], gs_send.at[t, slot], gs_recv.at[t - 1, slot], sibling
            ).wait_recv()

    groups = rows // 8

    def first_pass(t):
        start = 0 if t == 0 else 2 * t - 1
        count = 1 if t == 0 else 2
        n = count * rows
        span_k = slice(start * rows, start * rows + n)
        for i in range(count):
            key = window[start + i, 0]
            keys_x[(start + i) * rows:(start + i + 1) * rows, :HEAD] = key
            keys_t[:, (start + i) * rows:(start + i + 1) * rows] = key.T
        values = jnp.concatenate([window[start + i, 1] for i in range(count)], axis=0)
        if t == 0:
            key_at = lax.broadcasted_iota(jnp.int32, (rows, rows), 0)
            row_at = lax.broadcasted_iota(jnp.int32, (rows, rows), 1)
            causal = key_at <= row_at
        for h in range(heads):
            span = slice(h * rows, (h + 1) * rows)
            scores = jnp.dot(keys_x[span_k, :], q_t[:, span], preferred_element_type=F32)
            if t == 0:
                scores = jnp.where(causal, scores, -BIG)
            scores = scores.reshape(n // 8, 8, rows)
            top = jnp.max(scores, axis=0)
            top = jnp.broadcast_to(jnp.max(top, axis=0, keepdims=True), (8, rows))
            if t > 0:
                before = top_ref[h]
                top = jnp.maximum(before, top)
                shrink = jnp.exp2((before - top) * LOG2_SCALE)
            top_ref[h] = top
            snap_ref[t, h] = top
            p = jnp.exp2((scores - top[None]) * LOG2_SCALE)
            dp = jnp.dot(values, up_t[:, span], preferred_element_type=F32).reshape(n // 8, 8, rows)
            total = jnp.sum(p, axis=0)
            delta = jnp.sum(p * dp, axis=0)
            if t > 0:
                total = total + total_ref[h] * shrink
                delta = delta + delta_ref[h] * shrink
            total_ref[h] = total
            delta_ref[h] = delta
            if t == 0:
                p_a[h] = p.reshape(n, rows)
                dp_a[h] = dp.reshape(n, rows)
            else:
                p_b[t - 1, h] = p.reshape(n, rows)
                dp_b[t - 1, h] = dp.reshape(n, rows)

    give_z(0).wait_recv()

    @pl.when(core == 0)
    def _():
        copy(
            window.at[0, 1 - half], window.at[1, 1 - half], gs_send.at[0, 1], gs_recv.at[0, 1], sibling
        ).start()

    first_pass(0)
    relay_far(1)
    relay_far(2)
    relay_z(1)
    for t in range(1, PAIRS + 1):
        if t + 2 <= PAIRS:
            relay_far(t + 2)
        if t + 1 <= PAIRS:
            relay_z(t + 1)

        @pl.when(ctx >= 2 * t - 1)
        def _():
            await_sibling(t)

            @pl.when(ctx < 2 * t)
            def _():
                window[2 * t] = jnp.zeros((2, rows, HEAD), BF16)

            first_pass(t)

    for h in range(heads):
        inverse = 1.0 / jnp.broadcast_to(jnp.sum(total_ref[h], axis=0, keepdims=True), (8, rows))
        total_ref[h] = inverse
        delta_ref[h] = inverse * jnp.broadcast_to(
            jnp.sum(delta_ref[h], axis=0, keepdims=True), (8, rows)
        )

    def second_pass(t):
        start = 0 if t == 0 else 2 * t - 1
        count = 1 if t == 0 else 2
        n = count * rows
        span_k = slice(start * rows, start * rows + n)
        for h in range(heads):
            span = slice(h * rows, (h + 1) * rows)
            factor = jnp.exp2((snap_ref[t, h] - top_ref[h]) * LOG2_SCALE) * total_ref[h]
            p = p_a[h] if t == 0 else p_b[t - 1, h]
            dp = dp_a[h] if t == 0 else dp_b[t - 1, h]
            probs = p.reshape(n // 8, 8, rows) * factor[None]
            grads = probs * (dp.reshape(n // 8, 8, rows) - delta_ref[h][None])
            p16[:n, span] = probs.reshape(n, rows).astype(BF16)
            grad_s[span_k, span] = grads.reshape(n, rows).astype(BF16)
        grad_v = jnp.dot(p16[:n], up_n[...], preferred_element_type=F32)
        grad_k = jnp.dot(grad_s[span_k, :], q_n[...], preferred_element_type=F32) * SCALE
        if t == 0:
            part[0, 0] = grad_k
            part[0, 1] = grad_v
        else:
            sib_out[t - 1, 0] = grad_k[:rows]
            sib_out[t - 1, 1] = grad_v[:rows]
            part[t, 0] = grad_k[rows:]
            part[t, 1] = grad_v[rows:]

    def combine(e):
        def body():
            def add():
                send_sibling_recv(e)
                kept[e] = part[e, half] + sib_in[e, half]
                z_out[e] = (part[e, 1 - half] + sib_in[e, 1 - half]).astype(BF16)

            def alone():
                kept[e] = part[e, half]
                z_out[e] = part[e, 1 - half].astype(BF16)

            has = has_sibling_term(e)
            if has is None:
                add()
            else:
                pl.when(has)(add)
                pl.when(jnp.logical_not(has))(alone)
            send_z(e).start()

        if e == 0:
            body()
        else:
            pl.when(chip >= e)(body)

    def send_sibling_recv(e):
        copy(sib_out.at[0], sib_in.at[e], rs_send.at[0], rs_recv.at[e], sibling).wait_recv()

    def pass_on(e):
        @pl.when(chip >= e)
        def _():
            send_z(e).wait_recv()
            far_out[e - 1] = (kept[e] + z_in[e].astype(F32)).astype(BF16)
            send_far(e).start()

    def third_pass(h):
        cols = slice(h * rows, (h + 1) * rows)
        grad = jnp.dot(keys_t[...], grad_s[:, cols], preferred_element_type=F32)
        dq_ref[:, h * HEAD:(h + 1) * HEAD] = (grad.T * SCALE).astype(BF16)

    for t in range(PAIRS, 0, -1):
        @pl.when(ctx >= 2 * t - 1)
        def _():
            second_pass(t)
            send_sibling(t).start()

        @pl.when(ctx < 2 * t - 1)
        def _():
            span_k = slice((2 * t - 1) * rows, (2 * t + 1) * rows)
            grad_s[span_k, :] = jnp.zeros((2 * rows, all_rows), BF16)
            keys_t[:, span_k] = jnp.zeros((HEAD, 2 * rows), BF16)

        if t + 1 <= PAIRS:
            combine(t + 1)
        if t + 2 <= PAIRS:
            pass_on(t + 2)
    second_pass(0)
    combine(1)
    combine(0)
    pass_on(2)
    for h in range(heads // 2):
        third_pass(h)
    pass_on(1)
    for h in range(heads // 2, heads):
        third_pass(h)
    send_z(0).wait_recv()
    kept[0] = kept[0] + z_in[0].astype(F32)
    for e in range(PAIRS, 0, -1):
        @pl.when(chip + e < chips)
        def _():
            send_far(e).wait_recv()
            kept[0] = kept[0] + far_in[e - 1].astype(F32)
    dkv_ref[...] = kept[0].astype(BF16)

    for e in range(PAIRS + 1):
        @pl.when(chip >= e)
        def _():
            give_z(e).wait_send()
            send_z(e).wait_send()

        @pl.when(sibling_wants(e))
        def _():
            give_sibling(e, half, True).wait_send()
            give_sibling(e, 1 - half, False).wait_send()

        if e > 0:
            @pl.when(chip + e < chips)
            def _():
                give_far(e).wait_send()

            @pl.when(chip >= e)
            def _():
                send_far(e).wait_send()

            @pl.when(ctx >= 2 * e - 1)
            def _():
                send_sibling(e).wait_send()


def per_device(queries, upstream, key_value, doc_ids, seq_weight):
    rows, width = queries.shape
    heads = width // HEAD
    chips = lax.axis_size("ctx") // 2
    docs_n = seq_weight.shape[0]
    blocks = 2 * PAIRS + 1
    n = heads * rows
    vmem = pltpu.VMEM
    dma = pltpu.SemaphoreType.DMA
    whole = pl.BlockSpec(memory_space=pltpu.VMEM)
    scratch = [
        vmem((2 * HEAD, n), BF16),
        vmem((HEAD, n), BF16),
        vmem((n, HEAD), BF16),
        vmem((n, HEAD), BF16),
        vmem((blocks, 2, rows, HEAD), BF16),
        vmem((blocks * rows, 2 * HEAD), BF16),
        vmem((HEAD, blocks * rows), BF16),
        vmem((heads, rows, rows), F32),
        vmem((PAIRS, heads, 2 * rows, rows), F32),
        vmem((heads, rows, rows), F32),
        vmem((PAIRS, heads, 2 * rows, rows), F32),
        vmem((2 * rows, n), BF16),
        vmem((blocks * rows, n), BF16),
        vmem((heads, 8, rows), F32),
        vmem((PAIRS + 1, heads, 8, rows), F32),
        vmem((heads, 8, rows), F32),
        vmem((heads, 8, rows), F32),
        vmem((PAIRS + 1, 2, rows, HEAD), F32),
        vmem((PAIRS, 2, rows, HEAD), F32),
        vmem((PAIRS + 1, 2, rows, HEAD), F32),
        vmem((PAIRS + 1, rows, HEAD), F32),
        vmem((PAIRS + 1, rows, HEAD), BF16),
        vmem((PAIRS + 1, rows, HEAD), BF16),
        vmem((PAIRS, rows, HEAD), BF16),
        vmem((PAIRS, rows, HEAD), BF16),
        dma((PAIRS,)), dma((PAIRS,)),
        dma((PAIRS + 1,)), dma((PAIRS + 1,)),
        dma((PAIRS + 1, 2)), dma((PAIRS + 1, 2)),
        dma((PAIRS,)), dma((PAIRS + 1,)),
        dma((PAIRS + 1,)), dma((PAIRS + 1,)),
        dma((PAIRS,)), dma((PAIRS,)),
    ]
    return pl.pallas_call(
        functools.partial(kernel, rows, heads, chips, docs_n),
        out_shape=(
            jax.ShapeDtypeStruct(queries.shape, BF16),
            jax.ShapeDtypeStruct(key_value.shape, BF16),
        ),
        in_specs=[whole] * 4 + [pl.BlockSpec(memory_space=pltpu.SMEM)],
        out_specs=(whole, whole),
        scratch_shapes=scratch,
        compiler_params=pltpu.CompilerParams(
            collective_id=0, has_side_effects=True, vmem_limit_bytes=62 * 2**20
        ),
    )(queries, upstream, key_value, doc_ids.reshape(-1, 128), seq_weight)


def solution(mesh):
    return jax.shard_map(
        per_device,
        mesh=mesh,
        in_specs=(P("ctx", "head"), P("ctx", "head"), P("ctx", "head"), P(), P()),
        out_specs=(P("ctx", "head"), P("ctx", "head")),
        check_vma=False,
    )
```

time: 389 us -> 45 us (0.12)
  the two profiles are of different devices: /device:TPU:2 before, /device:TPU:68 now
where the time goes in v1:
time: 45 us; the launch traced here: 44.8 us
  Pallas kernels  41.6 us (92%)
  local copies, waits for them, and re-layouts  2.53 us (6%)
  between operations  0.65 us (1%)
    pallas_call x1, Pallas kernels, per_device(): pl.pallas_call(functools.partial(kernel, rows, heads, chips, docs_n), out...  41.6 us
    unnamed x4, local copies, waits for them, and re-layouts  2.53 us

profile of v1, /device:TPU:68, one launch (start us, length us, event | category | flops | bytes accessed | tf_op | source)
XLA Modules:
  0.0 44.8 jit_solution(10247946426458031499)
XLA Ops:
  0.6 41.6 %shard_map.68 = (bf16[256,1024]{1,0:T(8,128)(2,1)}, bf16[256,128]{1,0:T(8,128)(2,1)}) custom-call(bf16[256,1024]{1,0:T(8,128)(2,1)} %refs_0_.1, bf16[256,1024]{1,0:T(8,128)(2,1)} %refs_1_.1, bf16[256,128]{1,0:T(8,128)(2,1)} %refs_2_.1, s32[32,128]{1,0:T(8,128)} %bitcast.1, f32[4]{0:T(128)} %refs_4_.1), custom_call_target="tpu_custom_call" | custom-call | tf_op jit(solution)/shard_map/pallas_call | solution.py:414
  42.3 0.0 copy-start
  42.3 1.9 %copy.9 = bf16[256,1024]{1,0:T(8,128)(2,1)} copy(bf16[256,1024]{1,0:T(8,128)(2,1)} %get-tuple-element.4) | data formatting | bytes 1048576
  44.2 0.0 copy-done
  44.2 0.6 %copy.10 = bf16[256,128]{1,0:T(8,128)(2,1)} copy(bf16[256,128]{1,0:T(8,128)(2,1)S(1)} %copy-done) | data formatting | bytes 131072
Async XLA Ops:
  42.3 1.9 %copy-start = (bf16[256,128]{1,0:T(8,128)(2,1)S(1)}, bf16[256,128]{1,0:T(8,128)(2,1)}, u32[]{:S(2)}) copy-start(bf16[256,128]{1,0:T(8,128)(2,1)} %get-tuple-element.5) | copy-start | bytes 196612

commit v2 on v1

v2 whole, which is shorter than its diff:
```python
import functools
import math

import jax
import jax.numpy as jnp
from jax import lax
from jax.experimental import pallas as pl
from jax.experimental.pallas import tpu as pltpu
from jax.sharding import PartitionSpec as P

HEAD = 128
CHIPS_BACK = 4
GATHER_DIRECT = ()
REDUCE_DIRECT = ()
FAR_ORDER = (2, 4, 1, 3)
GATHER_SEQ = ("f4", "f2", "o0", "a0", "f1", "f3", "o4", "a4", "o2", "b4", "a2", "o1", "b2", "a1", "o3", "b1", "a3", "b3")
REDUCE_SEQ = (
    "s3", "s1", "c3", "s4", "c1", "s2", "c4", "g3", "s0", "c2", "g1", "c0",
    "q0", "q1", "q2", "q3", "g4", "q4", "q5", "g2", "q6", "q7",
)
FINAL_ORDER = (3, 1, 4, 2)
LOG2_SCALE = math.log2(math.e) / math.sqrt(HEAD)
SCALE = 1.0 / math.sqrt(HEAD)
BIG = 1e30
MESH = pl.DeviceIdType.MESH
F32 = jnp.float32
BF16 = jnp.bfloat16


def kernel(rows, heads, chips, docs_n, *refs):
    (
        q_hbm, up_hbm, kv_ref, docs_ref, weight_ref, dq_hbm, dkv_ref,
        q_ref, up_ref, dq_ref, q_t, up_t, q_n, up_n, window, keys_x, keys_t, p_s, dp_s, p16, grad_s,
        top_ref, snap_ref, total_ref, delta_ref,
        part, sib_out, sib_in, kept, z_out, z_in, far_out, far_in,
        local, gd_send, gd_recv, gz_send, gz_recv, gs_send, gs_recv,
        rs_send, rs_recv, rz_send, rz_recv, rd_send, rd_recv,
    ) = refs
    ctx = lax.axis_index("ctx")
    head = lax.axis_index("head")
    chip = ctx // 2
    core = ctx % 2
    half = head % 2
    sibling = (ctx + 1 - 2 * core, head)
    z_mate = (ctx, head + 1 - 2 * half)
    lines = rows // 128
    last = CHIPS_BACK

    def own_slot(e):
        return 0 if e == 0 else 2 * e - 1

    def sibling_slot(e):
        return 2 * last if e in (0, last) else 2 * e

    other = head + 1 - 2 * half
    direct_any = sorted(set(GATHER_DIRECT) | set(REDUCE_DIRECT))

    def later(e):
        return (ctx + 2 * e, head)

    def later_other(e):
        return (ctx + 2 * e, other)

    def earlier(e):
        return (ctx - 2 * e, head)

    def earlier_other(e):
        return (ctx - 2 * e, other)

    def copy(src, dst, send, recv, to):
        return pltpu.make_async_remote_copy(
            src_ref=src, dst_ref=dst, send_sem=send, recv_sem=recv, device_id=to, device_id_type=MESH
        )

    def has_earlier(e):
        return chip >= e

    def has_later(e):
        return chip + e < chips

    def give_far(e):
        return copy(
            kv_ref, window.at[own_slot(e), half], gd_send.at[e - 1], gd_recv.at[e - 1], later(e)
        )

    def give_other(e):
        return copy(
            kv_ref, window.at[own_slot(e), half], gz_send.at[e], gz_recv.at[e], later_other(e)
        )

    def give_z(e):
        src = kv_ref if e == 0 else window.at[own_slot(e), half]
        return copy(src, window.at[own_slot(e), half], gz_send.at[e], gz_recv.at[e], z_mate)

    def give_sibling(e, own):
        which = half if own else 1 - half
        src = kv_ref if own and e == 0 else window.at[own_slot(e), which]
        slot = 0 if own else 1
        at = last - 1 if e in (0, last) else e - 1
        return copy(
            src, window.at[sibling_slot(e), which], gs_send.at[e, slot], gs_recv.at[at, slot], sibling
        )

    def sibling_wants(e):
        if e == 0:
            return core == 0
        if e == last:
            return jnp.logical_and(has_earlier(e), core == 1)
        return has_earlier(e)

    def send_sibling(e):
        to = last - last * core if e == last else e
        return copy(sib_out.at[e - 1], sib_in.at[to], rs_send.at[e - 1], rs_recv.at[to], sibling)

    def await_sibling_term(e):
        copy(sib_out.at[0], sib_in.at[e], rs_send.at[0], rs_recv.at[e], sibling).wait_recv()

    def send_z(e):
        return copy(z_out.at[e], z_in.at[e], rz_send.at[e], rz_recv.at[e], z_mate)

    def send_far(e):
        return copy(far_out.at[e - 1], far_in.at[e - 1], rd_send.at[e - 1], rd_recv.at[e - 1], earlier(e))

    def send_other(e):
        return copy(z_out.at[e], z_in.at[e], rz_send.at[e], rz_recv.at[e], earlier_other(e))

    q_in = pltpu.make_async_copy(q_hbm, q_ref, local.at[0])
    up_in = pltpu.make_async_copy(up_hbm, up_ref, local.at[1])
    q_in.start()
    up_in.start()
    barrier = pltpu.get_barrier_semaphore()
    pl.semaphore_signal(barrier, inc=1, device_id=sibling, device_id_type=MESH)
    pl.semaphore_signal(barrier, inc=1, device_id=z_mate, device_id_type=MESH)
    for e in range(1, last + 1):
        @pl.when(has_later(e))
        def _():
            pl.semaphore_signal(barrier, inc=1, device_id=later(e), device_id_type=MESH)
            if e in direct_any:
                pl.semaphore_signal(barrier, inc=1, device_id=later_other(e), device_id_type=MESH)

        @pl.when(has_earlier(e))
        def _():
            pl.semaphore_signal(barrier, inc=1, device_id=earlier(e), device_id_type=MESH)
            if e in direct_any:
                pl.semaphore_signal(barrier, inc=1, device_id=earlier_other(e), device_id_type=MESH)

    window[0, half] = kv_ref[...]

    def doc_line(block):
        at = jnp.maximum(block, 0) * lines
        return jnp.concatenate([docs_ref[pl.ds(at + i, 1), :] for i in range(lines)], axis=1)

    sub = lax.broadcasted_iota(jnp.int32, (HEAD, rows), 0)
    row_docs = doc_line(ctx)
    row_weight = jnp.zeros((1, rows), F32)
    for d in range(docs_n):
        row_weight = row_weight + jnp.where(row_docs == d, weight_ref[d], 0.0)
    column_weight = jnp.broadcast_to(row_weight, (HEAD, rows)).T
    ban = jnp.where((sub < docs_n + 1) & (sub != row_docs), -BIG, 0.0).astype(BF16)

    partners = 2 + jnp.minimum(last, chips - 1 - chip) + jnp.minimum(last, chip)
    for e in direct_any:
        partners = partners + has_later(e).astype(jnp.int32) + has_earlier(e).astype(jnp.int32)
    pl.semaphore_wait(barrier, partners)

    give_z(0).start()
    for e in FAR_ORDER:
        @pl.when(has_later(e))
        def _():
            give_far(e).start()
            if e in GATHER_DIRECT:
                give_other(e).start()

    @pl.when(core == 0)
    def _():
        give_sibling(0, True).start()

    for slot in range(2 * last + 1):
        if slot == 2 * last:
            block = ctx - 1 - (2 * last - 2) * (1 - core)
        elif slot % 2 == 0 and slot > 0:
            block = ctx - slot + 1 - 2 * core
        else:
            block = ctx - (slot + 1) // 2 * 2
        key_docs = jnp.where(block >= 0, doc_line(block), docs_n)
        keys_x[slot * rows:(slot + 1) * rows, HEAD:] = jnp.where(sub == key_docs, 1.0, 0.0).astype(BF16).T

    q_in.wait()
    up_in.wait()
    for h in range(heads):
        cols = slice(h * HEAD, (h + 1) * HEAD)
        span = slice(h * rows, (h + 1) * rows)
        q_here = q_ref[:, cols]
        q_n[span, :] = q_here
        q_t[:HEAD, span] = q_here.T
        q_t[HEAD:, span] = ban
        weighted = (up_ref[:, cols].astype(F32) * column_weight).astype(BF16)
        up_n[span, :] = weighted
        up_t[:, span] = weighted.T

    def relay_far(e):
        @pl.when(has_earlier(e))
        def _():
            give_far(e).wait_recv()
            if e not in GATHER_DIRECT:
                give_z(e).start()

        @pl.when(sibling_wants(e))
        def _():
            give_sibling(e, True).start()

    def relay_other(e):
        if e == 0:
            give_z(0).wait_recv()
        else:
            @pl.when(has_earlier(e))
            def _():
                (give_other(e) if e in GATHER_DIRECT else give_z(e)).wait_recv()

        @pl.when(sibling_wants(e))
        def _():
            give_sibling(e, False).start()

    def await_sibling(e):
        for slot in range(2):
            copy(
                kv_ref, window.at[2 * e, 0], gs_send.at[e, slot], gs_recv.at[e - 1, slot], sibling
            ).wait_recv()

    groups = rows // 8

    def exists(e):
        return jnp.logical_or(chip >= e, core == 1) if e == last else chip >= e

    def first_pass(slot):
        first = slot == 0
        span_k = slice(slot * rows, (slot + 1) * rows)
        key = window[slot, 0]
        keys_x[span_k, :HEAD] = key
        keys_t[:, span_k] = key.T
        if first:
            key_at = lax.broadcasted_iota(jnp.int32, (rows, rows), 0)
            row_at = lax.broadcasted_iota(jnp.int32, (rows, rows), 1)
            causal = key_at <= row_at
        for h in range(heads):
            span = slice(h * rows, (h + 1) * rows)
            scores = jnp.dot(keys_x[span_k, :], q_t[:, span], preferred_element_type=F32)
            if first:
                scores = jnp.where(causal, scores, -BIG)
            scores = scores.reshape(groups, 8, rows)
            top = jnp.max(scores, axis=0)
            top = jnp.broadcast_to(jnp.max(top, axis=0, keepdims=True), (8, rows))
            if not first:
                before = top_ref[h]
                top = jnp.maximum(before, top)
                shrink = jnp.exp2((before - top) * LOG2_SCALE)
            top_ref[h] = top
            snap_ref[slot, h] = top
            p = jnp.exp2((scores - top[None]) * LOG2_SCALE)
            dp = jnp.dot(window[slot, 1], up_t[:, span], preferred_element_type=F32).reshape(groups, 8, rows)
            total = jnp.sum(p, axis=0)
            delta = jnp.sum(p * dp, axis=0)
            if not first:
                total = total + total_ref[h] * shrink
                delta = delta + delta_ref[h] * shrink
            total_ref[h] = total
            delta_ref[h] = delta
            p_s[slot, h] = p.reshape(rows, rows)
            dp_s[slot, h] = dp.reshape(rows, rows)

    def first_own(e):
        if e == 0:
            first_pass(0)
            return

        @pl.when(exists(e))
        def _():
            if e == last:
                @pl.when(chip < e)
                def _():
                    window[own_slot(e)] = jnp.zeros((2, rows, HEAD), BF16)

            first_pass(own_slot(e))

    def first_sibling(e):
        @pl.when(exists(e))
        def _():
            await_sibling(e)
            first_pass(2 * e)

    gather_step = {"f": relay_far, "o": relay_other, "a": first_own, "b": first_sibling}
    for step in GATHER_SEQ:
        gather_step[step[0]](int(step[1]))

    for h in range(heads):
        inverse = 1.0 / jnp.broadcast_to(jnp.sum(total_ref[h], axis=0, keepdims=True), (8, rows))
        total_ref[h] = inverse
        delta_ref[h] = inverse * jnp.broadcast_to(
            jnp.sum(delta_ref[h], axis=0, keepdims=True), (8, rows)
        )

    def second_pass(e):
        start = own_slot(e)
        count = 1 if e == 0 else 2
        n = count * rows
        span_k = slice(start * rows, start * rows + n)
        for i in range(count):
            for h in range(heads):
                span = slice(h * rows, (h + 1) * rows)
                factor = jnp.exp2((snap_ref[start + i, h] - top_ref[h]) * LOG2_SCALE) * total_ref[h]
                probs = p_s[start + i, h].reshape(groups, 8, rows) * factor[None]
                grads = probs * (dp_s[start + i, h].reshape(groups, 8, rows) - delta_ref[h][None])
                p16[i * rows:(i + 1) * rows, span] = probs.reshape(rows, rows).astype(BF16)
                here = (start + i) * rows
                grad_s[here:here + rows, span] = grads.reshape(rows, rows).astype(BF16)
        grad_v = jnp.dot(p16[:n], up_n[...], preferred_element_type=F32)
        grad_k = jnp.dot(grad_s[span_k, :], q_n[...], preferred_element_type=F32) * SCALE
        part[e, 0] = grad_k[:rows]
        part[e, 1] = grad_v[:rows]
        if e > 0:
            sib_out[e - 1, 0] = grad_k[rows:]
            sib_out[e - 1, 1] = grad_v[rows:]

    def second_stage(e):
        if e == 0:
            second_pass(0)
            return

        @pl.when(exists(e))
        def _():
            second_pass(e)
            send_sibling(e).start()

        @pl.when(jnp.logical_not(exists(e)))
        def _():
            span_k = slice(own_slot(e) * rows, (own_slot(e) + 2) * rows)
            grad_s[span_k, :] = jnp.zeros((2 * rows, heads * rows), BF16)
            keys_t[:, span_k] = jnp.zeros((HEAD, 2 * rows), BF16)

    def add_sibling_term(e):
        def add():
            await_sibling_term(e)
            part[e] = part[e] + sib_in[e]

        if e == 0:
            pl.when(core == 0)(add)
        elif e == last:
            pl.when(core == 1)(add)
        else:
            add()

    def combine(e):
        if e == 0:
            add_sibling_term(0)
            z_out[0] = part[0, 1 - half].astype(BF16)
            send_z(0).start()
            return

        @pl.when(has_earlier(e))
        def _():
            add_sibling_term(e)
            z_out[e] = part[e, 1 - half].astype(BF16)
            if e in REDUCE_DIRECT:
                send_other(e).start()
                far_out[e - 1] = part[e, half].astype(BF16)
                send_far(e).start()
            else:
                send_z(e).start()

    def pass_on(e):
        if e in REDUCE_DIRECT:
            return

        @pl.when(has_earlier(e))
        def _():
            send_z(e).wait_recv()
            far_out[e - 1] = (part[e, half] + z_in[e].astype(F32)).astype(BF16)
            send_far(e).start()

    def dq_out(h):
        cols = slice(h * HEAD, (h + 1) * HEAD)
        return pltpu.make_async_copy(dq_ref.at[:, cols], dq_hbm.at[:, cols], local.at[2 + h])

    def third_pass(h):
        cols = slice(h * rows, (h + 1) * rows)
        grad = jnp.dot(keys_t[...], grad_s[:, cols], preferred_element_type=F32)
        dq_ref[:, h * HEAD:(h + 1) * HEAD] = (grad.T * SCALE).astype(BF16)
        dq_out(h).start()

    reduce_step = {"s": second_stage, "c": combine, "g": pass_on, "q": third_pass}
    for step in REDUCE_SEQ:
        reduce_step[step[0]](int(step[1]))
    kept[...] = part[0, half]
    for e in FINAL_ORDER:
        @pl.when(has_later(e))
        def _():
            send_far(e).wait_recv()
            kept[...] = kept[...] + far_in[e - 1].astype(F32)
            if e in REDUCE_DIRECT:
                send_other(e).wait_recv()
                kept[...] = kept[...] + z_in[e].astype(F32)

    send_z(0).wait_recv()
    dkv_ref[...] = (kept[...] + z_in[0].astype(F32)).astype(BF16)

    for h in range(heads):
        dq_out(h).wait()
    give_z(0).wait_send()
    send_z(0).wait_send()
    for e in range(last + 1):
        @pl.when(sibling_wants(e))
        def _():
            give_sibling(e, True).wait_send()
            give_sibling(e, False).wait_send()

        if e > 0:
            @pl.when(has_later(e))
            def _():
                give_far(e).wait_send()
                if e in GATHER_DIRECT:
                    give_other(e).wait_send()

            @pl.when(has_earlier(e))
            def _():
                if e not in GATHER_DIRECT:
                    give_z(e).wait_send()
                send_far(e).wait_send()
                (send_other(e) if e in REDUCE_DIRECT else send_z(e)).wait_send()

            @pl.when(exists(e))
            def _():
                send_sibling(e).wait_send()


def per_device(queries, upstream, key_value, doc_ids, seq_weight):
    rows, width = queries.shape
    heads = width // HEAD
    chips = lax.axis_size("ctx") // 2
    docs_n = seq_weight.shape[0]
    last = CHIPS_BACK
    blocks = 2 * last + 1
    n = heads * rows
    vmem = pltpu.VMEM
    dma = pltpu.SemaphoreType.DMA
    whole = pl.BlockSpec(memory_space=pltpu.VMEM)
    hbm = pl.BlockSpec(memory_space=pl.ANY)
    scratch = [
        vmem(queries.shape, BF16),
        vmem(queries.shape, BF16),
        vmem(queries.shape, BF16),
        vmem((2 * HEAD, n), BF16),
        vmem((HEAD, n), BF16),
        vmem((n, HEAD), BF16),
        vmem((n, HEAD), BF16),
        vmem((blocks, 2, rows, HEAD), BF16),
        vmem((blocks * rows, 2 * HEAD), BF16),
        vmem((HEAD, blocks * rows), BF16),
        vmem((blocks, heads, rows, rows), F32),
        vmem((blocks, heads, rows, rows), F32),
        vmem((2 * rows, n), BF16),
        vmem((blocks * rows, n), BF16),
        vmem((heads, 8, rows), F32),
        vmem((blocks, heads, 8, rows), F32),
        vmem((heads, 8, rows), F32),
        vmem((heads, 8, rows), F32),
        vmem((last + 1, 2, rows, HEAD), F32),
        vmem((last, 2, rows, HEAD), F32),
        vmem((last + 1, 2, rows, HEAD), F32),
        vmem((rows, HEAD), F32),
        vmem((last + 1, rows, HEAD), BF16),
        vmem((last + 1, rows, HEAD), BF16),
        vmem((last, rows, HEAD), BF16),
        vmem((last, rows, HEAD), BF16),
        dma((2 + heads,)),
        dma((last,)), dma((last,)),
        dma((last + 1,)), dma((last + 1,)),
        dma((last + 1, 2)), dma((last, 2)),
        dma((last,)), dma((last + 1,)),
        dma((last + 1,)), dma((last + 1,)),
        dma((last,)), dma((last,)),
    ]
    grads = pl.pallas_call(
        functools.partial(kernel, rows, heads, chips, docs_n),
        out_shape=(
            jax.ShapeDtypeStruct(queries.shape, BF16),
            jax.ShapeDtypeStruct(key_value.shape, BF16),
        ),
        in_specs=[hbm, hbm, whole, whole, pl.BlockSpec(memory_space=pltpu.SMEM)],
        out_specs=(hbm, whole),
        scratch_shapes=scratch,
        compiler_params=pltpu.CompilerParams(
            collective_id=0, has_side_effects=True, vmem_limit_bytes=62 * 2**20
        ),
    )(queries, upstream, key_value, doc_ids.reshape(-1, 128), seq_weight)

    def settle(a, b, x, y):
        x[...] = a[...]
        y[...] = b[...]

    return pl.pallas_call(
        settle,
        out_shape=(
            jax.ShapeDtypeStruct(queries.shape, BF16),
            jax.ShapeDtypeStruct(key_value.shape, BF16),
        ),
        in_specs=[whole, whole],
        out_specs=(whole, whole),
    )(*grads)


def solution(mesh):
    return jax.shard_map(
        per_device,
        mesh=mesh,
        in_specs=(P("ctx", "head"), P("ctx", "head"), P("ctx", "head"), P(), P()),
        out_specs=(P("ctx", "head"), P("ctx", "head")),
        check_vma=False,
    )
```

time: 45 us -> 39.6 us (0.88)
  the two profiles are of different devices: /device:TPU:68 before, /device:TPU:2 now
where the time goes in v2:
time: 39.6 us; the launch traced here: 39.2 us
  Pallas kernels  38.6 us (97%)
  between operations  0.64 us (2%)
    pallas_call x1, Pallas kernels, per_device(): pl.pallas_call(functools.partial(kernel, rows, heads, chips, docs_n), out...  36.7 us
    pallas_call x1, Pallas kernels, per_device(): pl.pallas_call(settle, out_shape=(jax.ShapeDtypeStruct(queries.shape, BF1...  1.88 us

profile of v2, /device:TPU:2, one launch (start us, length us, event | category | flops | bytes accessed | tf_op | source)
XLA Modules:
  0.0 39.2 jit_solution(8288025748595929592)
XLA Ops:
  0.6 36.7 %shard_map.68 = (bf16[256,1024]{1,0:T(8,128)(2,1)}, bf16[256,128]{1,0:T(8,128)(2,1)}) custom-call(bf16[256,1024]{1,0:T(8,128)(2,1)} %refs_0_.1, bf16[256,1024]{1,0:T(8,128)(2,1)} %refs_1_.1, bf16[256,128]{1,0:T(8,128)(2,1)} %refs_2_.1, s32[32,128]{1,0:T(8,128)} %bitcast.1, f32[4]{0:T(128)} %refs_4_.1), custom_call_target="tpu_custom_call" | custom-call | tf_op jit(solution)/shard_map/pallas_call | solution.py:482
  37.4 1.9 %shard_map.69 = (bf16[256,1024]{1,0:T(8,128)(2,1)}, bf16[256,128]{1,0:T(8,128)(2,1)}) custom-call(bf16[256,1024]{1,0:T(8,128)(2,1)} %get-tuple-element.4.a, bf16[256,128]{1,0:T(8,128)(2,1)} %get-tuple-element.5.b), custom_call_target="tpu_custom_call" | custom-call | tf_op jit(solution)/shard_map/pallas_call | solution.py:500

commit v3 on v2

--- a/solution.py
+++ b/solution.py
@@ -10,12 +10,13 @@
 
 HEAD = 128
 CHIPS_BACK = 4
-GATHER_DIRECT = ()
-REDUCE_DIRECT = ()
-FAR_ORDER = (2, 4, 1, 3)
-GATHER_SEQ = ("f4", "f2", "o0", "a0", "f1", "f3", "o4", "a4", "o2", "b4", "a2", "o1", "b2", "a1", "o3", "b1", "a3", "b3")
+GATHER_BOTH = (2, 4)
+REDUCE_BOTH = ()
+FAR_EARLY = (1, 3)
+FAR_LATE = (2, 4)
+GATHER_SEQ = ("o0", "a0", "f1", "f3", "f2", "f4", "o1", "a1", "o2", "a2", "b1", "o4", "b2", "a4", "o3", "b4", "a3", "b3")
 REDUCE_SEQ = (
-    "s3", "s1", "c3", "s4", "c1", "s2", "c4", "g3", "s0", "c2", "g1", "c0",
+    "b3", "a3", "s1", "c3", "s4", "c1", "s2", "c4", "g3", "a0", "c2", "g1", "c0",
     "q0", "q1", "q2", "q3", "g4", "q4", "q5", "g2", "q6", "q7",
 )
 FINAL_ORDER = (3, 1, 4, 2)
@@ -52,20 +53,12 @@
     def sibling_slot(e):
         return 2 * last if e in (0, last) else 2 * e
 
-    other = head + 1 - 2 * half
-    direct_any = sorted(set(GATHER_DIRECT) | set(REDUCE_DIRECT))
 
     def later(e):
         return (ctx + 2 * e, head)
 
-    def later_other(e):
-        return (ctx + 2 * e, other)
-
     def earlier(e):
         return (ctx - 2 * e, head)
-
-    def earlier_other(e):
-        return (ctx - 2 * e, other)
 
     def copy(src, dst, send, recv, to):
         return pltpu.make_async_remote_copy(
@@ -85,7 +78,7 @@
 
     def give_other(e):
         return copy(
-            kv_ref, window.at[own_slot(e), half], gz_send.at[e], gz_recv.at[e], later_other(e)
+            window.at[0, 1 - half], window.at[own_slot(e), 1 - half], gz_send.at[e], gz_recv.at[e], later(e)
         )
 
     def give_z(e):
@@ -122,7 +115,7 @@
         return copy(far_out.at[e - 1], far_in.at[e - 1], rd_send.at[e - 1], rd_recv.at[e - 1], earlier(e))
 
     def send_other(e):
-        return copy(z_out.at[e], z_in.at[e], rz_send.at[e], rz_recv.at[e], earlier_other(e))
+        return copy(z_out.at[e], z_in.at[e], rz_send.at[e], rz_recv.at[e], earlier(e))
 
     q_in = pltpu.make_async_copy(q_hbm, q_ref, local.at[0])
     up_in = pltpu.make_async_copy(up_hbm, up_ref, local.at[1])
@@ -135,14 +128,10 @@
         @pl.when(has_later(e))
         def _():
             pl.semaphore_signal(barrier, inc=1, device_id=later(e), device_id_type=MESH)
-            if e in direct_any:
-                pl.semaphore_signal(barrier, inc=1, device_id=later_other(e), device_id_type=MESH)
 
         @pl.when(has_earlier(e))
         def _():
             pl.semaphore_signal(barrier, inc=1, device_id=earlier(e), device_id_type=MESH)
-            if e in direct_any:
-                pl.semaphore_signal(barrier, inc=1, device_id=earlier_other(e), device_id_type=MESH)
 
     window[0, half] = kv_ref[...]
 
@@ -159,17 +148,13 @@
     ban = jnp.where((sub < docs_n + 1) & (sub != row_docs), -BIG, 0.0).astype(BF16)
 
     partners = 2 + jnp.minimum(last, chips - 1 - chip) + jnp.minimum(last, chip)
-    for e in direct_any:
-        partners = partners + has_later(e).astype(jnp.int32) + has_earlier(e).astype(jnp.int32)
     pl.semaphore_wait(barrier, partners)
 
     give_z(0).start()
-    for e in FAR_ORDER:
+    for e in FAR_EARLY:
         @pl.when(has_later(e))
         def _():
             give_far(e).start()
-            if e in GATHER_DIRECT:
-                give_other(e).start()
 
     @pl.when(core == 0)
     def _():
@@ -198,11 +183,16 @@
         up_n[span, :] = weighted
         up_t[:, span] = weighted.T
 
+    for e in FAR_LATE:
+        @pl.when(has_later(e))
+        def _():
+            give_far(e).start()
+
     def relay_far(e):
         @pl.when(has_earlier(e))
         def _():
             give_far(e).wait_recv()
-            if e not in GATHER_DIRECT:
+            if e not in GATHER_BOTH:
                 give_z(e).start()
 
         @pl.when(sibling_wants(e))
@@ -212,10 +202,14 @@
     def relay_other(e):
         if e == 0:
             give_z(0).wait_recv()
+            for e_far in GATHER_BOTH:
+                @pl.when(has_later(e_far))
+                def _():
+                    give_other(e_far).start()
         else:
             @pl.when(has_earlier(e))
             def _():
-                (give_other(e) if e in GATHER_DIRECT else give_z(e)).wait_recv()
+                (give_other(e) if e in GATHER_BOTH else give_z(e)).wait_recv()
 
         @pl.when(sibling_wants(e))
         def _():
@@ -299,43 +293,60 @@
             jnp.sum(delta_ref[h], axis=0, keepdims=True), (8, rows)
         )
 
-    def second_pass(e):
-        start = own_slot(e)
-        count = 1 if e == 0 else 2
-        n = count * rows
-        span_k = slice(start * rows, start * rows + n)
+    def second_pass(start, count):
+        here = slice(start * rows, (start + count) * rows)
         for i in range(count):
+            slot = start + i
             for h in range(heads):
                 span = slice(h * rows, (h + 1) * rows)
-                factor = jnp.exp2((snap_ref[start + i, h] - top_ref[h]) * LOG2_SCALE) * total_ref[h]
-                probs = p_s[start + i, h].reshape(groups, 8, rows) * factor[None]
-                grads = probs * (dp_s[start + i, h].reshape(groups, 8, rows) - delta_ref[h][None])
+                factor = jnp.exp2((snap_ref[slot, h] - top_ref[h]) * LOG2_SCALE) * total_ref[h]
+                probs = p_s[slot, h].reshape(groups, 8, rows) * factor[None]
+                grads = probs * (dp_s[slot, h].reshape(groups, 8, rows) - delta_ref[h][None])
                 p16[i * rows:(i + 1) * rows, span] = probs.reshape(rows, rows).astype(BF16)
-                here = (start + i) * rows
-                grad_s[here:here + rows, span] = grads.reshape(rows, rows).astype(BF16)
-        grad_v = jnp.dot(p16[:n], up_n[...], preferred_element_type=F32)
-        grad_k = jnp.dot(grad_s[span_k, :], q_n[...], preferred_element_type=F32) * SCALE
-        part[e, 0] = grad_k[:rows]
-        part[e, 1] = grad_v[:rows]
-        if e > 0:
-            sib_out[e - 1, 0] = grad_k[rows:]
-            sib_out[e - 1, 1] = grad_v[rows:]
-
-    def second_stage(e):
+                grad_s[slot * rows:(slot + 1) * rows, span] = grads.reshape(rows, rows).astype(BF16)
+        grad_v = jnp.dot(p16[:count * rows], up_n[...], preferred_element_type=F32)
+        grad_k = jnp.dot(grad_s[here, :], q_n[...], preferred_element_type=F32) * SCALE
+        return grad_k, grad_v
+
+    def second_own(e):
+        def body():
+            grad_k, grad_v = second_pass(own_slot(e), 1)
+            part[e, 0] = grad_k
+            part[e, 1] = grad_v
+
         if e == 0:
-            second_pass(0)
-            return
-
-        @pl.when(exists(e))
-        def _():
-            second_pass(e)
-            send_sibling(e).start()
-
+            body()
+        else:
+            pl.when(exists(e))(body)
+
+    def second_missing(e):
         @pl.when(jnp.logical_not(exists(e)))
         def _():
             span_k = slice(own_slot(e) * rows, (own_slot(e) + 2) * rows)
             grad_s[span_k, :] = jnp.zeros((2 * rows, heads * rows), BF16)
             keys_t[:, span_k] = jnp.zeros((HEAD, 2 * rows), BF16)
+
+    def second_sibling(e):
+        @pl.when(exists(e))
+        def _():
+            grad_k, grad_v = second_pass(2 * e, 1)
+            sib_out[e - 1, 0] = grad_k
+            sib_out[e - 1, 1] = grad_v
+            send_sibling(e).start()
+
+        second_missing(e)
+
+    def second_pair(e):
+        @pl.when(exists(e))
+        def _():
+            grad_k, grad_v = second_pass(own_slot(e), 2)
+            sib_out[e - 1, 0] = grad_k[rows:]
+            sib_out[e - 1, 1] = grad_v[rows:]
+            send_sibling(e).start()
+            part[e, 0] = grad_k[:rows]
+            part[e, 1] = grad_v[:rows]
+
+        second_missing(e)
 
     def add_sibling_term(e):
         def add():
@@ -352,6 +363,12 @@
     def combine(e):
         if e == 0:
             add_sibling_term(0)
+            for e_far in REDUCE_BOTH:
+                @pl.when(has_later(e_far))
+                def _():
+                    send_other(e_far).wait_recv()
+                    part[0, 1 - half] = part[0, 1 - half] + z_in[e_far].astype(F32)
+
             z_out[0] = part[0, 1 - half].astype(BF16)
             send_z(0).start()
             return
@@ -360,7 +377,7 @@
         def _():
             add_sibling_term(e)
             z_out[e] = part[e, 1 - half].astype(BF16)
-            if e in REDUCE_DIRECT:
+            if e in REDUCE_BOTH:
                 send_other(e).start()
                 far_out[e - 1] = part[e, half].astype(BF16)
                 send_far(e).start()
@@ -368,7 +385,7 @@
                 send_z(e).start()
 
     def pass_on(e):
-        if e in REDUCE_DIRECT:
+        if e in REDUCE_BOTH:
             return
 
         @pl.when(has_earlier(e))
@@ -387,7 +404,7 @@
         dq_ref[:, h * HEAD:(h + 1) * HEAD] = (grad.T * SCALE).astype(BF16)
         dq_out(h).start()
 
-    reduce_step = {"s": second_stage, "c": combine, "g": pass_on, "q": third_pass}
+    reduce_step = {"a": second_own, "b": second_sibling, "s": second_pair, "c": combine, "g": pass_on, "q": third_pass}
     for step in REDUCE_SEQ:
         reduce_step[step[0]](int(step[1]))
     kept[...] = part[0, half]
@@ -396,9 +413,6 @@
         def _():
             send_far(e).wait_recv()
             kept[...] = kept[...] + far_in[e - 1].astype(F32)
-            if e in REDUCE_DIRECT:
-                send_other(e).wait_recv()
-                kept[...] = kept[...] + z_in[e].astype(F32)
 
     send_z(0).wait_recv()
     dkv_ref[...] = (kept[...] + z_in[0].astype(F32)).astype(BF16)
@@ -417,15 +431,15 @@
             @pl.when(has_later(e))
             def _():
                 give_far(e).wait_send()
-                if e in GATHER_DIRECT:
+                if e in GATHER_BOTH:
                     give_other(e).wait_send()
 
             @pl.when(has_earlier(e))
             def _():
-                if e not in GATHER_DIRECT:
+                if e not in GATHER_BOTH:
                     give_z(e).wait_send()
                 send_far(e).wait_send()
-                (send_other(e) if e in REDUCE_DIRECT else send_z(e)).wait_send()
+                (send_other(e) if e in REDUCE_BOTH else send_z(e)).wait_send()
 
             @pl.when(exists(e))
             def _():

time: 39.6 us -> 39.4 us (level)
  no operation moved by 1% of the time
where the time goes in v3:
time: 39.4 us; the launch traced here: 39.3 us
  Pallas kernels  38.6 us (98%)
  between operations  0.64 us (2%)
    pallas_call x1, Pallas kernels, per_device(): pl.pallas_call(functools.partial(kernel, rows, heads, chips, docs_n), out...  36.7 us
    pallas_call x1, Pallas kernels, per_device(): pl.pallas_call(settle, out_shape=(jax.ShapeDtypeStruct(queries.shape, BF1...  1.88 us

profile of v3, /device:TPU:2, one launch (start us, length us, event | category | flops | bytes accessed | tf_op | source)
XLA Modules:
  0.0 39.3 jit_solution(17376803441850926994)
XLA Ops:
  0.6 36.7 %shard_map.68 = (bf16[256,1024]{1,0:T(8,128)(2,1)}, bf16[256,128]{1,0:T(8,128)(2,1)}) custom-call(bf16[256,1024]{1,0:T(8,128)(2,1)} %refs_0_.1, bf16[256,1024]{1,0:T(8,128)(2,1)} %refs_1_.1, bf16[256,128]{1,0:T(8,128)(2,1)} %refs_2_.1, s32[32,128]{1,0:T(8,128)} %bitcast.1, f32[4]{0:T(128)} %refs_4_.1), custom_call_target="tpu_custom_call" | custom-call | tf_op jit(solution)/shard_map/pallas_call | solution.py:496
  37.4 1.9 %shard_map.69 = (bf16[256,1024]{1,0:T(8,128)(2,1)}, bf16[256,128]{1,0:T(8,128)(2,1)}) custom-call(bf16[256,1024]{1,0:T(8,128)(2,1)} %get-tuple-element.4.a, bf16[256,128]{1,0:T(8,128)(2,1)} %get-tuple-element.5.b), custom_call_target="tpu_custom_call" | custom-call | tf_op jit(solution)/shard_map/pallas_call | solution.py:514
